TPU v7x, 32 devices: a whole 2x2x4 slice. The times are simulated.
32 devices in a mesh: dp: 4 (over z), proto: 8 (over y, x, core).
Axes of the slice: x: 2, y: 2, z: 4, core: 2. Of those that a mesh axis runs over, the one named last changes fastest.
Arguments:
- embeddings: bfloat16 [8192, 2560], P('proto', 'dp'), may hold values from -26 to 26
- table: bfloat16 [32768, 2560], P('proto', 'dp'), may hold values from -5 to 5
- tile_lists: int32 [8, 8], replicated, may hold values from 0 to 255, as said below
- labels: int32 [8192], P('proto'), may hold values from 0 to 32767, as said below
Outputs:
- loss: float32 [], replicated
- grad_emb: bfloat16 [8192, 2560], P('proto', 'dp')
- grad_table: bfloat16 [32768, 2560], P('proto', 'dp')
Inputs may be any that keep to these rules, and one draw needn't show every extreme that they name: `tile_lists`: each block's 8 tile ids are distinct and fall on exactly 4 owners (owner = id // 32), each of those owners holding exactly 2 of them. `labels`: the tile of each row's label (label // 128) is in the list of the row's block.
All inputs are finite; a program needn't handle non-finite values.
Results may differ from a plain program's by a relative error of at most 0.0025.
The roundings to bfloat16 on the way count: a program that leaves them out, or rounds other values in their place, can miss the bound.
Values may be sent and summed in bfloat16 or wider, within the bound.
A program may use at most 128 MiB of HBM per device.

v0:
```python
import math
import jax
import jax.numpy as jnp
from jax import lax
from jax.sharding import PartitionSpec as P

D = 2560
TILE = 128
CAP = 2


def slot_plan(ids, tiles_here):
    owners = ids // tiles_here
    local = ids % tiles_here
    count = ids.shape[-1]
    before = jnp.arange(count)[:, None] > jnp.arange(count)[None, :]
    earlier = (owners[..., :, None] == owners[..., None, :]) & before
    rank = jnp.sum(earlier.astype(jnp.int32), axis=-1)
    return (owners, local, rank)


def softmax_terms(scores, ids, lab, list_len):
    hit = (ids[None, :] == (lab // TILE)[:, None]).astype(jnp.int32)
    column = (
        jnp.sum(hit * (jnp.arange(list_len, dtype=jnp.int32) * TILE)[None, :], axis=1) + lab % TILE
    )
    onehot = (jnp.arange(list_len * TILE, dtype=jnp.int32)[None, :] == column[:, None]).astype(
        jnp.float32
    )
    top = jnp.max(scores, axis=1, keepdims=True)
    expo = jnp.exp(scores - top)
    total = jnp.sum(expo, axis=1, keepdims=True)
    lse = top[:, 0] + jnp.log(total[:, 0])
    target = jnp.sum(scores * onehot, axis=1)
    dz_rows = (expo / total - onehot).astype(jnp.bfloat16)
    return (jnp.sum(lse - target), dz_rows)


def body(embeddings, table, tile_lists, labels):
    block_rows, width = embeddings.shape
    list_len = tile_lists.shape[1]
    tiles_here = table.shape[0] // TILE
    groups = lax.axis_size("proto")
    dp_count = lax.axis_size("dp")
    rows_dev = block_rows // dp_count
    total_rows = block_rows * groups
    me = lax.axis_index("proto")
    part = lax.axis_index("dp")
    inv_scale = 1.0 / math.sqrt(D)
    owners, local, rank = slot_plan(tile_lists, tiles_here)
    match = (owners == me)[:, :, None] & (
        rank[:, :, None] == jnp.arange(CAP, dtype=jnp.int32)[None, None, :]
    )
    select = jnp.sum(match.astype(jnp.int32) * local[:, :, None], axis=1)
    shaped_table = table.reshape(tiles_here, TILE, width)
    outgoing = jnp.take(shaped_table, select.reshape(-1), axis=0).reshape(groups, CAP, TILE, width)
    incoming = lax.all_to_all(outgoing, "proto", split_axis=0, concat_axis=0, tiled=True)
    my_ids = lax.dynamic_index_in_dim(tile_lists, me, 0, keepdims=False)
    my_owner = lax.dynamic_index_in_dim(owners, me, 0, keepdims=False)
    my_rank = lax.dynamic_index_in_dim(rank, me, 0, keepdims=False)
    flat_slot = my_owner * CAP + my_rank
    tiles = jnp.take(incoming.reshape(groups * CAP, TILE, width), flat_slot, axis=0).reshape(
        list_len * TILE, width
    )
    scores = (
        lax.psum_scatter(
            lax.dot_general(
                embeddings, tiles, (((1,), (1,)), ((), ())), preferred_element_type=jnp.float32
            ),
            "dp",
            scatter_dimension=0,
            tiled=True,
        )
        * inv_scale
    )
    my_labels = lax.dynamic_slice_in_dim(labels, part * rows_dev, rows_dev, 0)
    loss_part, dz_rows = softmax_terms(scores, my_ids, my_labels, list_len)
    dz_block = lax.all_gather(dz_rows, "dp", axis=0, tiled=True)
    loss = lax.psum(loss_part, ("dp", "proto")) / total_rows
    grad_emb = jnp.dot(dz_block, tiles, preferred_element_type=jnp.float32).astype(jnp.bfloat16)
    piece = lax.dot_general(
        dz_block, embeddings, (((0,), (0,)), ((), ())), preferred_element_type=jnp.float32
    ).astype(jnp.bfloat16)
    returning = (
        jnp.zeros((groups * CAP, TILE, width), jnp.bfloat16)
        .at[flat_slot]
        .set(piece.reshape(list_len, TILE, width))
    )
    returned = lax.all_to_all(
        returning.reshape(groups, CAP, TILE, width),
        "proto",
        split_axis=0,
        concat_axis=0,
        tiled=True,
    )
    accum = (
        jnp.zeros((tiles_here, TILE, width), jnp.float32)
        .at[select.reshape(-1)]
        .add(returned.reshape(groups * CAP, TILE, width))
    )
    grad_table = accum.reshape(tiles_here * TILE, width).astype(jnp.bfloat16)
    return (loss, grad_emb, grad_table)


def solution(mesh):
    placed = (P("proto", "dp"), P("proto", "dp"), P(), P("proto"))
    return jax.shard_map(
        body,
        mesh=mesh,
        in_specs=placed,
        out_specs=(P(), P("proto", "dp"), P("proto", "dp")),
        check_vma=False,
    )
```

profile of v0, /device:TPU:0, one launch (start us, length us, event | category | flops | bytes accessed | tf_op | source)
XLA Modules:
  0.0 308.0 jit_solution(9859530231807013274)
XLA Ops:
  7.2 0.0 copy-start
  7.2 0.8 add_select_fusion
  8.0 0.7 broadcast_compare_fusion
  8.7 0.3 convert_reduce_fusion
  9.0 0.2 select_reduce_fusion.2
  9.1 0.1 copy.8
  9.2 0.1 copy.7
  9.3 0.1 reshape.136
  9.4 4.8 %gather_fusion = bf16[16,128,640]{2,1,0:T(8,128)(2,1)} fusion(bf16[32,128,640]{2,1,0:T(8,128)(2,1)} %bitcast.36, s32[1024]{0:T(1024)S(1)} %pad_clamp_fusion.1), kind=kCustom, calls=%fused_computation | custom fusion | bytes 5242944 | tf_op jit(solution)/shard_map/jit(_take)/gather | solution.py:56
  14.3 3.6 %broadcast_select_fusion = bf16[8,2,128,640]{3,2,1,0:T(8,128)(2,1)} fusion(bf16[8,2,128,640]{3,2,1,0:T(8,128)(2,1)} %bitcast.33, pred[8,2]{1,0:T(8,128)(4,1)S(1)} %copy.7), kind=kLoop, calls=%fused_computation.5 | loop fusion | flops 1310720 | bytes 5242896 | tf_op jit(solution)/shard_map/jit(_take)/select_n | solution.py:56
  17.8 5.2 %all-to-all-start = ((bf16[8,2,128,640]{3,2,1,0:T(8,128)(2,1)}), bf16[8,2,128,640]{3,2,1,0:T(8,128)(2,1)}, u32[]{:S(2)}, u32[]{:S(2)}) async-start(bf16[8,2,128,640]{3,2,1,0:T(8,128)(2,1)} %broadcast_select_fusion), calls=%async_computation | async-start | bytes 5242880 | tf_op jit(solution)/shard_map/all_to_all | solution.py:57
  23.0 0.0 reduce-scatter.2.cloned.1.call-start
  23.1 0.1 broadcast_bitcast_fusion
  23.2 32.2 %all-to-all-done = bf16[8,2,128,640]{3,2,1,0:T(8,128)(2,1)} async-done(((bf16[8,2,128,640]{3,2,1,0:T(8,128)(2,1)}), bf16[8,2,128,640]{3,2,1,0:T(8,128)(2,1)}, u32[]{:S(2)}, u32[]{:S(2)}) %all-to-all-start) | async-done | bytes 2621472 | tf_op jit(solution)/shard_map/all_to_all | solution.py:57
  55.4 2.5 gather_fusion.1
  57.9 0.3 bitcast_select_fusion
  58.2 0.0 copy-start.2
  58.2 1.0 copy-done.2
  59.3 0.0 copy-done
  59.3 3.8 %convolution_bitcast_fusion = f32[1024,1024]{0,1:T(8,128)} fusion(bf16[1024,640]{1,0:T(8,128)(2,1)S(1)} %bitcast_select_fusion, bf16[1024,640]{1,0:T(8,128)(2,1)S(1)} %copy-done), kind=kOutput, calls=%fused_computation.6 | convolution fusion | flops 1342177280 | bytes 6815744 | tf_op jit(solution)/shard_map/dot_general | solution.py:67
  63.1 0.0 copy-start.4
  63.1 0.0 reduce-scatter.2.cloned.1.call-update
  63.2 0.0 all-gather.2.cloned.1.call-start
  63.2 0.7 fusion.7
  63.9 0.0 copy-done.4
  63.9 0.1 and_select_fusion.1
  64.0 0.1 select_reduce_fusion.1
  64.1 0.1 fusion.4
  64.2 75.9 %reduce-scatter.2.cloned.1.call-done = f32[256,1024]{0,1:T(8,128)} async-done(((f32[1024,1024]{0,1:T(8,128)}), f32[256,1024]{0,1:T(8,128)}) %reduce-scatter.2.cloned.1.call-update) | async-done | bytes 1048592 | tf_op jit(solution)/shard_map/reduce_scatter | solution.py:66
  140.1 1.5 multiply_reduce_fusion
  141.6 1.5 fusion
  143.1 0.0 copy-done.1
  143.1 1.1 subtract_convert_fusion
  144.3 0.0 all-gather.2.cloned.1.call-update
  144.3 46.9 %all-gather.2.cloned.1.call-done = bf16[1024,1024]{0,1:T(8,128)(2,1)} async-done(((bf16[256,1024]{0,1:T(8,128)(2,1)}), bf16[1024,1024]{0,1:T(8,128)(2,1)}) %all-gather.2.cloned.1.call-update) | async-done | bytes 2097168 | tf_op jit(solution)/shard_map/all_gather | solution.py:78
  191.2 3.4 %convolution_convert_fusion = bf16[1024,640]{1,0:T(8,128)(2,1)S(1)} fusion(bf16[1024,1024]{0,1:T(8,128)(2,1)} %all-gather.2.cloned.1.call-done, bf16[1024,640]{1,0:T(8,128)(2,1)S(1)} %copy-done), kind=kOutput, calls=%fused_computation.7 | convolution fusion | flops 1342832640 | bytes 4718592 | tf_op jit(solution)/shard_map/dot_general | solution.py:81
  194.6 1.8 broadcast_in_dim.55
  196.4 3.1 scatter_fusion
  199.4 4.5 %all-to-all-start.1 = ((bf16[8,2,128,640]{3,2,1,0:T(8,128)(2,1)}), bf16[8,2,128,640]{3,2,1,0:T(8,128)(2,1)}, u32[]{:S(2)}, u32[]{:S(2)}) async-start(bf16[8,2,128,640]{3,2,1,0:T(8,128)(2,1)} %bitcast.32), calls=%async_computation.2 | async-start | bytes 5242880 | tf_op jit(solution)/shard_map/all_to_all | solution.py:89
  203.9 0.6 subtract_reduce_fusion
  204.5 62.9 %psum.7 = f32[]{:T(128)} all-reduce(f32[]{:T(128)} %subtract_reduce_fusion), channel_id=1, replica_groups=mesh['dp'=4,'proto'=8] {'dp','proto'}, use_global_device_ids=true, to_apply=%region_8.9 | all-reduce | flops 1 | bytes 8 | tf_op jit(solution)/shard_map/psum | solution.py:79
  268.1 0.0 copy-done.3
  268.1 4.5 %convolution_convert_fusion.1 = bf16[1024,640]{1,0:T(8,128)(2,1)} fusion(bf16[1024,1024]{0,1:T(8,128)(2,1)} %all-gather.2.cloned.1.call-done, bf16[1024,640]{1,0:T(8,128)(2,1)S(1)} %copy-done.3), kind=kOutput, calls=%fused_computation.8 | convolution fusion | flops 1342832640 | bytes 4718592 | tf_op jit(solution)/shard_map/dot_general | solution.py:80
  272.6 0.0 all-to-all-done.1
  272.6 4.6 %bitcast_convert_fusion = f32[16,128,640]{2,1,0:T(8,128)} fusion(bf16[8,2,128,640]{3,2,1,0:T(8,128)(2,1)} %all-to-all-done.1), kind=kLoop, calls=%fused_computation.4 | loop fusion | flops 1310720 | bytes 7864320 | tf_op jit(solution)/shard_map/convert_element_type | solution.py:99
  277.3 5.2 %broadcast_in_dim.54 = f32[32,128,640]{2,1,0:T(8,128)} broadcast(f32[]{:T(128)} %constant.115.clone.1), dimensions={} | broadcast | bytes 10485764 | tf_op jit(solution)/shard_map/broadcast_in_dim | solution.py:97
  282.5 10.5 %scatter_fusion.1 = f32[32,128,640]{2,1,0:T(8,128)} fusion(f32[32,128,640]{2,1,0:T(8,128)} %broadcast_in_dim.54, s32[16]{0:T(128)S(1)} %fusion.8, f32[16,128,640]{2,1,0:T(8,128)} %bitcast_convert_fusion), kind=kCustom, calls=%fused_computation.3 | custom fusion | flops 1310720 | bytes 15728704 | tf_op jit(solution)/shard_map/scatter-add | solution.py:99
  292.9 7.1 %convert_element_type.36 = bf16[32,128,640]{2,1,0:T(8,128)(2,1)} convert(f32[32,128,640]{2,1,0:T(8,128)} %scatter_fusion.1) | non-fusion elementwise | flops 2621440 | bytes 15728640 | tf_op jit(solution)/shard_map/convert_element_type | solution.py:101
  (9 shorter events, 0.1 us)
Async XLA Ops:
  7.2 52.1 %copy-start = (bf16[1024,640]{1,0:T(8,128)(2,1)S(1)}, bf16[1024,640]{1,0:T(8,128)(2,1)}, u32[]{:S(2)}) copy-start(bf16[1024,640]{1,0:T(8,128)(2,1)} %param.4) | copy-start | bytes 3932164
  17.8 37.5 %all-to-all-start = ((bf16[8,2,128,640]{3,2,1,0:T(8,128)(2,1)}), bf16[8,2,128,640]{3,2,1,0:T(8,128)(2,1)}, u32[]{:S(2)}, u32[]{:S(2)}) async-start(bf16[8,2,128,640]{3,2,1,0:T(8,128)(2,1)} %broadcast_select_fusion), calls=%async_computation | async-start | bytes 5242880 | tf_op jit(solution)/shard_map/all_to_all | solution.py:57
  23.0 117.1 %reduce-scatter.2.cloned.1.call-start = ((), (), s32[]{:S(2)}) async-start(), calls=%async_computation.3 | async-start | bytes 5242880 | tf_op jit(solution)/shard_map/reduce_scatter | solution.py:66
  58.2 1.1 copy-start.2
  63.1 0.8 copy-start.4
  63.2 128.0 %all-gather.2.cloned.1.call-start = ((), (), s32[]{:S(2)}) async-start(), calls=%async_computation.4 | async-start | bytes 2621440 | tf_op jit(solution)/shard_map/all_gather | solution.py:78
  140.1 3.0 copy-start.1
  199.4 68.7 %copy-start.3 = (bf16[1024,640]{1,0:T(8,128)(2,1)S(1)}, bf16[1024,640]{1,0:T(8,128)(2,1)}, u32[]{:S(2)}) copy-start(bf16[1024,640]{1,0:T(8,128)(2,1)} %copy-done.2) | copy-start | bytes 3932164
  199.4 73.2 %all-to-all-start.1 = ((bf16[8,2,128,640]{3,2,1,0:T(8,128)(2,1)}), bf16[8,2,128,640]{3,2,1,0:T(8,128)(2,1)}, u32[]{:S(2)}, u32[]{:S(2)}) async-start(bf16[8,2,128,640]{3,2,1,0:T(8,128)(2,1)} %bitcast.32), calls=%async_computation.2 | async-start | bytes 5242880 | tf_op jit(solution)/shard_map/all_to_all | solution.py:89
Sparse Core Ops, SparseCore 0:
  63.3 76.7 reduce-scatter.1
  144.4 46.7 all-gather.1
where the time goes:
time: 309 us; the launch traced here: 308 us
  waiting for transfers between devices  155 us (50%)
  blocking collectives  62.9 us (20%)
  other arithmetic  33.1 us (11%)
  local copies, waits for them, and re-layouts  19.5 us (6%)
  between operations  15.9 us (5%)
  matrix products  11.7 us (4%)
  starting transfers between devices  9.76 us (3%)
    reduce_scatter x1, waiting for transfers between devices, body(): lax.psum_scatter(lax.dot_general(embeddings, tiles, (((1,), (1,)), ((), (...  75.9 us
    psum x1, blocking collectives, body(): loss = lax.psum(loss_part, ('dp', 'proto')) / total_rows  62.9 us
    all_gather x1, waiting for transfers between devices, body(): dz_block = lax.all_gather(dz_rows, 'dp', axis=0, tiled=True)  46.9 us
    all_to_all x1, waiting for transfers between devices, body(): lax.all_to_all(outgoing, 'proto', split_axis=0, concat_axis=0, tiled=True)  32.2 us
    scatter-add x1, other arithmetic, body(): accum = jnp.zeros((tiles_here, TILE, width), jnp.float32).at[select.resha...  10.5 us
    convert_element_type x1, other arithmetic, body(): grad_table = accum.reshape(tiles_here * TILE, width).astype(jnp.bfloat16)  7.1 us
  transfers between devices with their start and end apart: 4, of which 3 were waited for; matrix products, arithmetic and copies ran while one was open for 2% of the time, Pallas kernels for 0%

commit v1 on v0

--- a/solution.py
+++ b/solution.py
@@ -7,6 +7,22 @@
 D = 2560
 TILE = 128
 CAP = 2
+
+
+def exchange_in_pairs(x, axis, split, join):
+    ways, here = (lax.axis_size(axis), lax.axis_index(axis))
+    width = x.shape[split] // ways
+    shape = list(x.shape)
+    shape[split] = width
+    height = shape[join]
+    shape[join] = height * ways
+    full = jnp.zeros(shape, x.dtype)
+    for mask in range(ways):
+        part = lax.dynamic_slice_in_dim(x, (here ^ mask) * width, width, axis=split)
+        if mask:
+            part = lax.ppermute(part, axis, [(d, d ^ mask) for d in range(ways)])
+        full = lax.dynamic_update_slice_in_dim(full, part, (here ^ mask) * height, axis=join)
+    return full
 
 
 def slot_plan(ids, tiles_here):
@@ -54,7 +70,7 @@
     select = jnp.sum(match.astype(jnp.int32) * local[:, :, None], axis=1)
     shaped_table = table.reshape(tiles_here, TILE, width)
     outgoing = jnp.take(shaped_table, select.reshape(-1), axis=0).reshape(groups, CAP, TILE, width)
-    incoming = lax.all_to_all(outgoing, "proto", split_axis=0, concat_axis=0, tiled=True)
+    incoming = exchange_in_pairs(outgoing, "proto", 0, 0)
     my_ids = lax.dynamic_index_in_dim(tile_lists, me, 0, keepdims=False)
     my_owner = lax.dynamic_index_in_dim(owners, me, 0, keepdims=False)
     my_rank = lax.dynamic_index_in_dim(rank, me, 0, keepdims=False)

time: 309 us -> 318 us (1.029)
  local copies, waits for them, and re-layouts: 19.5 us -> 27.6 us
    ppermute x0 -> x7, waiting for transfers between devices: none -> 32.6 us  [exchange_in_pairs(): part = lax.ppermute(part, axis, [(d, d ^ mask) for d in range(ways)])]
    all_to_all x1 -> x0, waiting for transfers between devices: 32.2 us -> none  [body(): lax.all_to_all(outgoing, 'proto', split_axis=0, concat_axis=0, tiled=True)]
    ppermute x0 -> x7, starting transfers between devices: none -> 7.55 us  [exchange_in_pairs(): part = lax.ppermute(part, axis, [(d, d ^ mask) for d in range(ways)])]
    dynamic_update_slice x0 -> x7, local copies, waits for them, and re-layouts: none -> 5.27 us  [exchange_in_pairs(): lax.dynamic_update_slice_in_dim(full, part, (here ^ mask) * height, axis=...]
    all_to_all x1 -> x0, starting transfers between devices: 5.17 us -> none  [body(): lax.all_to_all(outgoing, 'proto', split_axis=0, concat_axis=0, tiled=True)]
  transfers between devices with their start and end apart: 4 -> 10, of which waited for: 3 -> 5; matrix products, arithmetic and copies ran while one was open for 2% -> 3% of each run, Pallas kernels for 0% -> 0%
where the time goes in v1:
time: 318 us
  waiting for transfers between devices  156 us (49%)
  blocking collectives  62.9 us (20%)
  other arithmetic  31.6 us (10%)
  local copies, waits for them, and re-layouts  27.6 us (9%)
  between operations  16 us (5%)
  starting transfers between devices  12.1 us (4%)
  matrix products  11.7 us (4%)
    reduce_scatter x1, waiting for transfers between devices, body(): lax.psum_scatter(lax.dot_general(embeddings, tiles, (((1,), (1,)), ((), (...  76.3 us
    psum x1, blocking collectives, body(): loss = lax.psum(loss_part, ('dp', 'proto')) / total_rows  62.9 us
    all_gather x1, waiting for transfers between devices, body(): dz_block = lax.all_gather(dz_rows, 'dp', axis=0, tiled=True)  46.9 us
    ppermute x7, waiting for transfers between devices, exchange_in_pairs(): part = lax.ppermute(part, axis, [(d, d ^ mask) for d in range(ways)])  32.6 us
    scatter-add x1, other arithmetic, body(): accum = jnp.zeros((tiles_here, TILE, width), jnp.float32).at[select.resha...  10.5 us
    ppermute x7, starting transfers between devices, exchange_in_pairs(): part = lax.ppermute(part, axis, [(d, d ^ mask) for d in range(ways)])  7.55 us
    convert_element_type x1, other arithmetic, body(): grad_table = accum.reshape(tiles_here * TILE, width).astype(jnp.bfloat16)  7.1 us
  transfers between devices with their start and end apart: 10, of which 5 were waited for; matrix products, arithmetic and copies ran while one was open for 3% of the time, Pallas kernels for 0%

profile of v1, /device:TPU:0, one launch (start us, length us, event | category | flops | bytes accessed | tf_op | source)
XLA Modules:
  0.0 317.7 jit_solution(11610583997041148877)
XLA Ops:
  7.3 0.8 add_select_fusion
  8.0 0.7 broadcast_compare_fusion
  8.7 0.3 convert_reduce_fusion
  9.0 0.2 select_reduce_fusion.2
  9.3 0.1 copy.7
  9.5 4.8 %gather_fusion = bf16[16,128,640]{2,1,0:T(8,128)(2,1)} fusion(bf16[32,128,640]{2,1,0:T(8,128)(2,1)} %bitcast.36, s32[1024]{0:T(1024)S(1)} %pad_clamp_fusion.1), kind=kCustom, calls=%fused_computation | custom fusion | bytes 5242944 | tf_op jit(solution)/shard_map/jit(_take)/gather | solution.py:72
  14.4 2.1 broadcast_select_fusion
  16.4 1.8 broadcast_in_dim.54
  18.2 1.0 constant_dynamic-slice_fusion.1
  19.2 3.3 %collective-permute-start.6 = (bf16[1,2,128,640]{3,2,1,0:T(8,128)(2,1)S(1)}, bf16[1,2,128,640]{3,2,1,0:T(8,128)(2,1)S(1)}, u32[]{:S(2)}, u32[]{:S(2)}) collective-permute-start(bf16[1,2,128,640]{3,2,1,0:T(8,128)(2,1)S(1)} %get-tuple-element.9), channel_id=1, source_target_pairs={{0,7},{1,6},{2,5},{3,4},{4,3},{5,2},{6,1},{7,0},{8,15},{9,14},{10,... | collective-permute-start | bytes 983048 | tf_op jit(solution)/shard_map/ppermute | solution.py:23
  22.6 0.6 collective-permute-start.5
  23.1 1.4 collective-permute-start.2
  24.6 0.3 collective-permute-start.1
  24.9 0.2 collective-permute-start
  25.1 1.4 collective-permute-done
  26.5 1.7 collective-permute-start.3
  28.2 0.8 constant_dynamic-update-slice_fusion.6
  29.0 23.7 %collective-permute-done.1 = bf16[1,2,128,640]{3,2,1,0:T(8,128)(2,1)S(1)} collective-permute-done((bf16[1,2,128,640]{3,2,1,0:T(8,128)(2,1)S(1)}, bf16[1,2,128,640]{3,2,1,0:T(8,128)(2,1)S(1)}, u32[]{:S(2)}, u32[]{:S(2)}) %collective-permute-start.1) | collective-permute-done | bytes 327712 | tf_op jit(solution)/shard_map/ppermute | solution.py:23
  52.7 0.8 constant_dynamic-update-slice_fusion.5
  53.5 0.8 constant_dynamic-update-slice_fusion.4
  54.3 0.8 constant_dynamic-update-slice_fusion.3
  55.0 7.5 %collective-permute-done.4 = bf16[1,2,128,640]{3,2,1,0:T(8,128)(2,1)S(1)} collective-permute-done((bf16[1,2,128,640]{3,2,1,0:T(8,128)(2,1)S(1)}, bf16[1,2,128,640]{3,2,1,0:T(8,128)(2,1)S(1)}, u32[]{:S(2)}, u32[]{:S(2)}) %collective-permute-start.4) | collective-permute-done | bytes 327712 | tf_op jit(solution)/shard_map/ppermute | solution.py:23
  62.5 0.8 constant_dynamic-update-slice_fusion.2
  63.2 0.8 constant_dynamic-update-slice_fusion.1
  64.0 0.8 constant_dynamic-update-slice_fusion
  64.7 2.5 gather_fusion.1
  67.3 0.3 bitcast_select_fusion
  67.6 1.0 copy-done.2
  68.7 3.8 %convolution_bitcast_fusion = f32[1024,1024]{0,1:T(8,128)} fusion(bf16[1024,640]{1,0:T(8,128)(2,1)S(1)} %bitcast_select_fusion, bf16[1024,640]{1,0:T(8,128)(2,1)S(1)} %copy-done), kind=kOutput, calls=%fused_computation.6 | convolution fusion | flops 1342177280 | bytes 6815744 | tf_op jit(solution)/shard_map/dot_general | solution.py:83
  72.6 0.7 fusion.9
  73.4 0.1 select_reduce_fusion.1
  73.5 0.1 fusion.4
  73.5 76.3 %reduce-scatter.2.cloned.1.call-done = f32[256,1024]{0,1:T(8,128)} async-done(((f32[1024,1024]{0,1:T(8,128)}), f32[256,1024]{0,1:T(8,128)}) %reduce-scatter.2.cloned.1.call-update) | async-done | bytes 1048592 | tf_op jit(solution)/shard_map/reduce_scatter | solution.py:82
  149.8 1.5 multiply_reduce_fusion
  151.3 1.5 fusion
  152.8 1.1 subtract_convert_fusion
  154.0 46.9 %all-gather.2.cloned.1.call-done = bf16[1024,1024]{0,1:T(8,128)(2,1)} async-done(((bf16[256,1024]{0,1:T(8,128)(2,1)}), bf16[1024,1024]{0,1:T(8,128)(2,1)}) %all-gather.2.cloned.1.call-update) | async-done | bytes 2097168 | tf_op jit(solution)/shard_map/all_gather | solution.py:94
  200.9 3.4 %convolution_convert_fusion = bf16[1024,640]{1,0:T(8,128)(2,1)S(1)} fusion(bf16[1024,1024]{0,1:T(8,128)(2,1)} %all-gather.2.cloned.1.call-done, bf16[1024,640]{1,0:T(8,128)(2,1)S(1)} %copy-done), kind=kOutput, calls=%fused_computation.7 | convolution fusion | flops 1342832640 | bytes 4718592 | tf_op jit(solution)/shard_map/dot_general | solution.py:97
  204.3 1.8 broadcast_in_dim.59
  206.1 3.1 scatter_fusion
  209.1 4.5 %all-to-all-start = ((bf16[8,2,128,640]{3,2,1,0:T(8,128)(2,1)}), bf16[8,2,128,640]{3,2,1,0:T(8,128)(2,1)}, u32[]{:S(2)}, u32[]{:S(2)}) async-start(bf16[8,2,128,640]{3,2,1,0:T(8,128)(2,1)} %bitcast.32), calls=%async_computation.1 | async-start | bytes 5242880 | tf_op jit(solution)/shard_map/all_to_all | solution.py:105
  213.6 0.6 subtract_reduce_fusion
  214.3 62.9 %psum.7 = f32[]{:T(128)} all-reduce(f32[]{:T(128)} %subtract_reduce_fusion), channel_id=1, replica_groups=mesh['dp'=4,'proto'=8] {'dp','proto'}, use_global_device_ids=true, to_apply=%region_8.9 | all-reduce | flops 1 | bytes 8 | tf_op jit(solution)/shard_map/psum | solution.py:95
  277.8 4.5 %convolution_convert_fusion.1 = bf16[1024,640]{1,0:T(8,128)(2,1)} fusion(bf16[1024,1024]{0,1:T(8,128)(2,1)} %all-gather.2.cloned.1.call-done, bf16[1024,640]{1,0:T(8,128)(2,1)S(1)} %copy-done.3), kind=kOutput, calls=%fused_computation.8 | convolution fusion | flops 1342832640 | bytes 4718592 | tf_op jit(solution)/shard_map/dot_general | solution.py:96
  282.3 4.6 %bitcast_convert_fusion = f32[16,128,640]{2,1,0:T(8,128)} fusion(bf16[8,2,128,640]{3,2,1,0:T(8,128)(2,1)} %all-to-all-done), kind=kLoop, calls=%fused_computation.4 | loop fusion | flops 1310720 | bytes 7864320 | tf_op jit(solution)/shard_map/convert_element_type | solution.py:115
  287.0 5.2 %broadcast_in_dim.58 = f32[32,128,640]{2,1,0:T(8,128)} broadcast(f32[]{:T(128)} %constant.129.clone.1), dimensions={} | broadcast | bytes 10485764 | tf_op jit(solution)/shard_map/broadcast_in_dim | solution.py:113
  292.2 10.5 %scatter_fusion.1 = f32[32,128,640]{2,1,0:T(8,128)} fusion(f32[32,128,640]{2,1,0:T(8,128)} %broadcast_in_dim.58, s32[16]{0:T(128)S(1)} %fusion.5, f32[16,128,640]{2,1,0:T(8,128)} %bitcast_convert_fusion), kind=kCustom, calls=%fused_computation.3 | custom fusion | flops 1310720 | bytes 15728704 | tf_op jit(solution)/shard_map/scatter-add | solution.py:115
  302.6 7.1 %convert_element_type.36 = bf16[32,128,640]{2,1,0:T(8,128)(2,1)} convert(f32[32,128,640]{2,1,0:T(8,128)} %scatter_fusion.1) | non-fusion elementwise | flops 2621440 | bytes 15728640 | tf_op jit(solution)/shard_map/convert_element_type | solution.py:117
  (30 shorter events, 0.5 us)
Async XLA Ops:
  7.2 61.5 %copy-start = (bf16[1024,640]{1,0:T(8,128)(2,1)S(1)}, bf16[1024,640]{1,0:T(8,128)(2,1)}, u32[]{:S(2)}) copy-start(bf16[1024,640]{1,0:T(8,128)(2,1)} %param.4) | copy-start | bytes 3932164
  7.2 142.6 %reduce-scatter.2.cloned.1.call-start = ((), (), s32[]{:S(2)}) async-start(), calls=%async_computation.2 | async-start | bytes 5242880 | tf_op jit(solution)/shard_map/reduce_scatter | solution.py:82
  19.2 44.8 %collective-permute-start.6 = (bf16[1,2,128,640]{3,2,1,0:T(8,128)(2,1)S(1)}, bf16[1,2,128,640]{3,2,1,0:T(8,128)(2,1)S(1)}, u32[]{:S(2)}, u32[]{:S(2)}) collective-permute-start(bf16[1,2,128,640]{3,2,1,0:T(8,128)(2,1)S(1)} %get-tuple-element.9), channel_id=1, source_target_pairs={{0,7},{1,6},{2,5},{3,4},{4,3},{5,2},{6,1},{7,0},{8,15},{9,14},{10,... | collective-permute-start | bytes 983048 | tf_op jit(solution)/shard_map/ppermute | solution.py:23
  22.6 40.7 %collective-permute-start.5 = (bf16[1,2,128,640]{3,2,1,0:T(8,128)(2,1)S(1)}, bf16[1,2,128,640]{3,2,1,0:T(8,128)(2,1)S(1)}, u32[]{:S(2)}, u32[]{:S(2)}) collective-permute-start(bf16[1,2,128,640]{3,2,1,0:T(8,128)(2,1)S(1)} %get-tuple-element.10), channel_id=1, source_target_pairs={{0,6},{1,7},{2,4},{3,5},{4,2},{5,3},{6,0},{7,1},{8,14},{9,15},{10,... | collective-permute-start | bytes 983048 | tf_op jit(solution)/shard_map/ppermute | solution.py:23
  23.1 30.4 %collective-permute-start.2 = (bf16[1,2,128,640]{3,2,1,0:T(8,128)(2,1)S(1)}, bf16[1,2,128,640]{3,2,1,0:T(8,128)(2,1)S(1)}, u32[]{:S(2)}, u32[]{:S(2)}) collective-permute-start(bf16[1,2,128,640]{3,2,1,0:T(8,128)(2,1)S(1)} %get-tuple-element.13), channel_id=1, source_target_pairs={{0,3},{1,2},{2,1},{3,0},{4,7},{5,6},{6,5},{7,4},{8,11},{9,10},{10,... | collective-permute-start | bytes 983048 | tf_op jit(solution)/shard_map/ppermute | solution.py:23
  24.6 28.2 %collective-permute-start.1 = (bf16[1,2,128,640]{3,2,1,0:T(8,128)(2,1)S(1)}, bf16[1,2,128,640]{3,2,1,0:T(8,128)(2,1)S(1)}, u32[]{:S(2)}, u32[]{:S(2)}) collective-permute-start(bf16[1,2,128,640]{3,2,1,0:T(8,128)(2,1)S(1)} %get-tuple-element.14), channel_id=1, source_target_pairs={{0,2},{1,3},{2,0},{3,1},{4,6},{5,7},{6,4},{7,5},{8,10},{9,11},{10,... | collective-permute-start | bytes 983048 | tf_op jit(solution)/shard_map/ppermute | solution.py:23
  24.9 1.6 collective-permute-start
  26.5 27.8 %collective-permute-start.3 = (bf16[1,2,128,640]{3,2,1,0:T(8,128)(2,1)S(1)}, bf16[1,2,128,640]{3,2,1,0:T(8,128)(2,1)S(1)}, u32[]{:S(2)}, u32[]{:S(2)}) collective-permute-start(bf16[1,2,128,640]{3,2,1,0:T(8,128)(2,1)S(1)} %get-tuple-element.12), channel_id=1, source_target_pairs={{0,4},{1,5},{2,6},{3,7},{4,0},{5,1},{6,2},{7,3},{8,12},{9,13},{10,... | collective-permute-start | bytes 983048 | tf_op jit(solution)/shard_map/ppermute | solution.py:23
  52.7 9.7 %collective-permute-start.4 = (bf16[1,2,128,640]{3,2,1,0:T(8,128)(2,1)S(1)}, bf16[1,2,128,640]{3,2,1,0:T(8,128)(2,1)S(1)}, u32[]{:S(2)}, u32[]{:S(2)}) collective-permute-start(bf16[1,2,128,640]{3,2,1,0:T(8,128)(2,1)S(1)} %get-tuple-element.11), channel_id=1, source_target_pairs={{0,5},{1,4},{2,7},{3,6},{4,1},{5,0},{6,3},{7,2},{8,13},{9,12},{10,... | collective-permute-start | bytes 983048 | tf_op jit(solution)/shard_map/ppermute | solution.py:23
  67.6 1.1 copy-start.2
  72.5 0.8 copy-start.4
  72.5 128.4 %all-gather.2.cloned.1.call-start = ((), (), s32[]{:S(2)}) async-start(), calls=%async_computation.3 | async-start | bytes 2621440 | tf_op jit(solution)/shard_map/all_gather | solution.py:94
  149.8 3.0 copy-start.1
  209.1 68.7 %copy-start.3 = (bf16[1024,640]{1,0:T(8,128)(2,1)S(1)}, bf16[1024,640]{1,0:T(8,128)(2,1)}, u32[]{:S(2)}) copy-start(bf16[1024,640]{1,0:T(8,128)(2,1)} %copy-done.2) | copy-start | bytes 3932164
  209.1 73.2 %all-to-all-start = ((bf16[8,2,128,640]{3,2,1,0:T(8,128)(2,1)}), bf16[8,2,128,640]{3,2,1,0:T(8,128)(2,1)}, u32[]{:S(2)}, u32[]{:S(2)}) async-start(bf16[8,2,128,640]{3,2,1,0:T(8,128)(2,1)} %bitcast.32), calls=%async_computation.1 | async-start | bytes 5242880 | tf_op jit(solution)/shard_map/all_to_all | solution.py:105
Sparse Core Ops, SparseCore 0:
  72.6 77.1 reduce-scatter.1
  154.1 46.7 all-gather.1
